TPU v7x, 1024 devices: a whole 4x4x32 slice. The times are simulated.
1024 devices in a mesh: row: 64 (over x, z_lo, core), col: 16 (over y, z_hi).
Axes of the slice: x: 4, y: 4, z: 32 (z_hi: 4, z_lo: 8; z = z_hi * 8 + z_lo), core: 2. Of those that a mesh axis runs over, the one named last changes fastest.
Arguments:
- hamilton: bfloat16 [4096, 4096], P('row', 'col'), may hold values from -17 to 17, as said below
- block_flags: int32 [64, 64], P('row', 'col'), may hold values from 0 to 1, as said below
Outputs:
- next_iterate: float32 [4096, 4096], P('row', 'col')
Inputs may be any that keep to these rules, and one draw needn't show every extreme that they name: The hamilton matrix is real and symmetric. `block_flags`: block i sits at cell (p_i // 16, p_i % 16) of a periodic grid of 4 by 16 cells, where p is a permutation of the block indices; a block is kept only if both periodic cell distances between its row and column blocks are at most 2, and always if both are at most 1. The flags are symmetric.
All inputs are finite; a program needn't handle non-finite values.
Results may differ from a plain program's by a relative error of at most 0.0052.
Values may be sent and summed in bfloat16 or wider, within the bound.
A program may use at most 32 MiB of HBM per device.

v0:
```python
import jax
import jax.numpy as jnp
from jax import lax
from jax.sharding import PartitionSpec as P


def widen(block_flags, size):
    return jnp.repeat(jnp.repeat(block_flags, size, 0), size, 1)


def body(hamilton, block_flags):
    size = hamilton.shape[0] // block_flags.shape[0]
    keeper = widen(block_flags, size) > 0
    masked = jnp.where(keeper, hamilton, jnp.zeros_like(hamilton))
    wide = masked.astype(jnp.float32)
    squares = lax.psum(jnp.sum(wide * wide), ("row", "col"))
    order = hamilton.shape[1] * lax.axis_size("col")
    factor = jnp.sqrt(jnp.float32(order) / squares)
    xmat = (wide * factor).astype(jnp.bfloat16)
    panel = lax.all_gather(xmat, "col", axis=1, tiled=True)
    left_part = panel
    first = jnp.dot(
        left_part,
        lax.all_gather(xmat, "row", axis=0, tiled=True),
        preferred_element_type=jnp.float32,
    ).astype(jnp.bfloat16)
    square_rows = lax.all_gather(first, "col", axis=1, tiled=True)
    left_part = square_rows
    second = jnp.dot(
        left_part,
        lax.all_gather(xmat, "row", axis=0, tiled=True),
        preferred_element_type=jnp.float32,
    )
    return 16.0 * (1.5 * xmat.astype(jnp.float32) - 0.5 * second)


def solution(mesh):
    in_specs = (P("row", "col"), P("row", "col"))
    out_specs = P("row", "col")
    return jax.shard_map(body, mesh=mesh, in_specs=in_specs, out_specs=out_specs, check_vma=False)
```

profile of v0, /device:TPU:4, one launch (start us, length us, event | category | flops | bytes accessed | tf_op | source)
XLA Modules:
  0.0 430.0 jit_solution(4465755141351523192)
XLA Ops:
  6.5 0.0 all-gather.2.cloned.1.call-start
  6.5 0.7 compare_bitcast_fusion
  7.2 0.1 broadcast_in_dim.9
  7.3 0.1 gt.17
  7.4 1.4 fusion.2
  8.7 168.0 %psum.7 = f32[]{:T(128)} all-reduce(f32[]{:T(128)} %fusion.2), channel_id=1, replica_groups=mesh['row'=64,'col'=16] {'row','col'}, use_global_device_ids=true, to_apply=%region_1.2 | all-reduce | flops 1 | bytes 8 | tf_op jit(solution)/shard_map/psum | solution.py:16
  177.4 1.4 fusion.3
  178.8 0.0 copy-start.1
  178.8 0.0 all-gather.2.cloned.1.call-update
  178.8 83.5 %all_gather.10 = bf16[64,4096]{1,0:T(8,128)(2,1)S(1)} all-gather(bf16[64,256]{1,0:T(8,128)(2,1)} %fusion.3), channel_id=1, replica_groups=mesh['row'=64,'col'=16] {'col'}, dimensions={1}, use_global_device_ids=true | all-gather | bytes 557056 | tf_op jit(solution)/shard_map/all_gather | solution.py:20
  262.3 46.6 %all-gather.2.cloned.1.call-done = bf16[4096,256]{1,0:T(8,128)(2,1)} async-done(((bf16[64,256]{1,0:T(8,128)(2,1)}), bf16[4096,256]{1,0:T(8,128)(2,1)}) %all-gather.2.cloned.1.call-update) | async-done | bytes 2097168 | tf_op jit(solution)/shard_map/all_gather | solution.py:24
  308.9 0.0 copy-start
  308.9 2.2 convolution_convert_fusion
  311.1 111.0 %all_gather.12 = bf16[64,4096]{1,0:T(8,128)(2,1)S(1)} all-gather(bf16[64,256]{1,0:T(8,128)(2,1)S(1)} %convolution_convert_fusion), channel_id=1, replica_groups=mesh['row'=64,'col'=16] {'col'}, dimensions={1}, use_global_device_ids=true | all-gather | bytes 557056 | tf_op jit(solution)/shard_map/all_gather | solution.py:27
  422.1 0.0 copy-done.1
  422.1 0.0 copy-done
  422.1 1.1 fusion.1
Async XLA Ops:
  6.5 302.4 %all-gather.2.cloned.1.call-start = ((), (), s32[]{:S(2)}) async-start(), calls=%async_computation | async-start | bytes 2129920 | tf_op jit(solution)/shard_map/all_gather | solution.py:24
  178.8 243.3 %copy-start.1 = (bf16[64,256]{1,0:T(8,128)(2,1)S(1)}, bf16[64,256]{1,0:T(8,128)(2,1)}, u32[]{:S(2)}) copy-start(bf16[64,256]{1,0:T(8,128)(2,1)} %fusion.3) | copy-start | bytes 98308
  308.9 113.2 %copy-start = (bf16[4096,256]{1,0:T(8,128)(2,1)S(1)}, bf16[4096,256]{1,0:T(8,128)(2,1)}, u32[]{:S(2)}) copy-start(bf16[4096,256]{1,0:T(8,128)(2,1)} %all-gather.2.cloned.1.call-done) | copy-start | bytes 6291460
Sparse Core Ops, SparseCore 0:
  179.0 129.8 all-gather.1
where the time goes:
time: 430 us
  blocking collectives  362 us (84%)
  waiting for transfers between devices  46.6 us (11%)
  between operations  14.1 us (3%)
    psum x1, blocking collectives, body(): squares = lax.psum(jnp.sum(wide * wide), ('row', 'col'))  168 us
    all_gather x1, blocking collectives, body(): square_rows = lax.all_gather(first, 'col', axis=1, tiled=True)  111 us
    all_gather x1, blocking collectives, body(): panel = lax.all_gather(xmat, 'col', axis=1, tiled=True)  83.5 us
    all_gather x1, waiting for transfers between devices, body(): lax.all_gather(xmat, 'row', axis=0, tiled=True)  46.6 us
  transfers between devices with their start and end apart: 1, of which 1 were waited for; matrix products, arithmetic and copies ran while one was open for 0% of the time, Pallas kernels for 0%

commit v1 on v0

v1 whole, which is shorter than its diff:
```python
import jax
import jax.numpy as jnp
from jax import lax
from jax.experimental import pallas as pl
from jax.experimental.pallas import tpu as pltpu
from jax.sharding import PartitionSpec as P

MESH = pl.DeviceIdType.MESH
NX, NY, NZL, NZH, NC = 4, 4, 8, 4, 2
BS = 64
WIDE = 256
ORDER = 4096


def kernel(flag_ref, h_ref, out_ref, panel, rowp, firstp, xpanel, p1, p2, p3, send, recv):
    row = lax.axis_index("row")
    col = lax.axis_index("col")
    x = lax.div(row, NZL * NC)
    zl = lax.rem(lax.div(row, NC), NZL)
    c = lax.rem(row, NC)
    y = lax.div(col, NZH)
    zh = lax.rem(col, NZH)

    def dev(x=x, y=y, zl=zl, zh=zh, c=c):
        return ((x * NZL + zl) * NC + c, y * NZH + zh)

    def zl_peer(d):
        return dev(zl=lax.rem(zl + d, NZL))

    def zh_peer(d):
        return dev(zh=lax.rem(zh + d, NZH))

    def x_peer(d):
        return dev(x=lax.rem(x + d, NX))

    def y_peer(d):
        return dev(y=lax.rem(y + d, NY))

    def xc_peer(d):
        at = lax.rem(x * NC + c + d, NX * NC)
        return dev(x=lax.div(at, NC), c=lax.rem(at, NC))

    def col_peer(d):
        at = lax.rem(col + d, NY * NZH)
        return (row, at)

    other = dev(c=1 - c)

    barrier = pltpu.get_barrier_semaphore()

    def greet(count, peer):
        def step(d, carry):
            pl.semaphore_signal(barrier, inc=1, device_id=peer(d), device_id_type=MESH)
            return carry

        lax.fori_loop(1, count, step, 0)

    greet(NX * NC, xc_peer)
    greet(NZL, zl_peer)
    greet(NY * NZH, col_peer)

    def spread(count, peer, ref, k):
        def step(d, carry):
            pltpu.make_async_remote_copy(
                src_ref=ref,
                dst_ref=ref,
                send_sem=send.at[k],
                recv_sem=recv.at[k],
                device_id=peer(d),
                device_id_type=MESH,
            ).start()
            return carry

        lax.fori_loop(1, count, step, 0)

    def await_bytes(view, sem):
        pltpu.make_async_copy(view, view, sem).wait()

    total = jnp.zeros((1, 128), jnp.float32)
    for b in range(4):
        part = h_ref[:, b * BS:(b + 1) * BS]
        part = jnp.where(flag_ref[0, b] > 0, part, jnp.zeros_like(part))
        panel[x, zl, c, :, b * BS:(b + 1) * BS] = part
        rowp[y, zh, :, b * BS:(b + 1) * BS] = part
    wide = rowp[y, zh].astype(jnp.float32)
    wide = wide * wide
    half = wide[:, :128] + wide[:, 128:]
    total = jnp.sum(half, axis=0, keepdims=True)
    p1[x * NC + c] = total

    pl.semaphore_wait(barrier, (NX * NC - 1) + (NZL - 1) + (NY * NZH - 1))

    spread(NX * NC, xc_peer, p1.at[x * NC + c], 0)
    spread(NZH, zh_peer, rowp.at[y, zh], 1)
    spread(NZL, zl_peer, panel.at[x, zl, c], 2)

    await_bytes(p1.at[pl.ds(0, 7)], recv.at[0])
    p2[zl] = jnp.sum(p1[...], axis=0)
    spread(NZL, zl_peer, p2.at[zl], 3)
    await_bytes(p2.at[pl.ds(0, 7)], recv.at[3])
    p3[col] = jnp.sum(p2[...], axis=0)
    spread(NY * NZH, col_peer, p3.at[col], 4)

    await_bytes(rowp.at[0, pl.ds(0, 3)], recv.at[1])
    spread(NY, y_peer, rowp.at[y], 5)
    await_bytes(panel.at[0, pl.ds(0, 7), 0], recv.at[2])
    spread(NX, x_peer, panel.at[x, :, c], 6)

    def across(ref, k):
        copy = pltpu.make_async_remote_copy(
            src_ref=ref,
            dst_ref=ref,
            send_sem=send.at[k],
            recv_sem=recv.at[k],
            device_id=other,
            device_id_type=MESH,
        )
        copy.start()

    across(panel.at[x, :, c], 7)

    await_bytes(p3.at[pl.ds(0, 15)], recv.at[4])
    squares = jnp.sum(jnp.sum(p3[...], axis=0), axis=1, keepdims=True)
    factor = jnp.sqrt(jnp.float32(ORDER) / squares)

    await_bytes(panel.at[pl.ds(0, 3), :, 0], recv.at[6])
    for d in range(1, NX):
        at = lax.rem(x + d, NX)
        across(panel.at[at, :, c], 7 + d)
    await_bytes(rowp.at[pl.ds(0, 3)], recv.at[5])
    for d in range(NX):
        await_bytes(panel.at[0, :, 0], recv.at[7 + d])

    acc = jnp.zeros((BS, WIDE), jnp.float32)
    for j in range(16):
        left = (rowp[j // 4, j % 4].astype(jnp.float32) * factor).astype(jnp.bfloat16)
        chunk = panel[j // 4, (j % 4) * 2:(j % 4) * 2 + 2].reshape(WIDE, WIDE)
        right = (chunk.astype(jnp.float32) * factor).astype(jnp.bfloat16)
        xpanel[j] = right
        acc += jnp.dot(left, right, preferred_element_type=jnp.float32)
    firstp[y, zh] = acc.astype(jnp.bfloat16)

    spread(NZH, zh_peer, firstp.at[y, zh], 11)
    await_bytes(firstp.at[0, pl.ds(0, 3)], recv.at[11])
    spread(NY, y_peer, firstp.at[y], 12)
    await_bytes(firstp.at[pl.ds(0, 3)], recv.at[12])

    acc = jnp.zeros((BS, WIDE), jnp.float32)
    for j in range(16):
        acc += jnp.dot(firstp[j // 4, j % 4], xpanel[j], preferred_element_type=jnp.float32)
    own = (rowp[y, zh].astype(jnp.float32) * factor).astype(jnp.bfloat16).astype(jnp.float32)
    out_ref[...] = 16.0 * (1.5 * own - 0.5 * acc)

    await_bytes(p1.at[pl.ds(0, 7)], send.at[0])
    await_bytes(rowp.at[0, pl.ds(0, 3)], send.at[1])
    await_bytes(panel.at[0, pl.ds(0, 7), 0], send.at[2])
    await_bytes(p2.at[pl.ds(0, 7)], send.at[3])
    await_bytes(p3.at[pl.ds(0, 15)], send.at[4])
    await_bytes(rowp.at[pl.ds(0, 3)], send.at[5])
    await_bytes(panel.at[pl.ds(0, 3), :, 0], send.at[6])
    for d in range(NX):
        await_bytes(panel.at[0, :, 0], send.at[7 + d])
    await_bytes(firstp.at[0, pl.ds(0, 3)], send.at[11])
    await_bytes(firstp.at[pl.ds(0, 3)], send.at[12])


def body(hamilton, block_flags):
    return pl.pallas_call(
        kernel,
        out_shape=jax.ShapeDtypeStruct((BS, WIDE), jnp.float32),
        in_specs=[
            pl.BlockSpec(memory_space=pltpu.SMEM),
            pl.BlockSpec(memory_space=pltpu.VMEM),
        ],
        out_specs=pl.BlockSpec(memory_space=pltpu.VMEM),
        scratch_shapes=[
            pltpu.VMEM((NX, NZL, NC, BS, WIDE), jnp.bfloat16),
            pltpu.VMEM((NY, NZH, BS, WIDE), jnp.bfloat16),
            pltpu.VMEM((NY, NZH, BS, WIDE), jnp.bfloat16),
            pltpu.VMEM((16, WIDE, WIDE), jnp.bfloat16),
            pltpu.VMEM((8, 1, 128), jnp.float32),
            pltpu.VMEM((8, 1, 128), jnp.float32),
            pltpu.VMEM((16, 1, 128), jnp.float32),
            pltpu.SemaphoreType.DMA((13,)),
            pltpu.SemaphoreType.DMA((13,)),
        ],
        compiler_params=pltpu.CompilerParams(
            collective_id=0, has_side_effects=True, vmem_limit_bytes=32 * 1024 * 1024
        ),
    )(block_flags, hamilton)


def solution(mesh):
    in_specs = (P("row", "col"), P("row", "col"))
    out_specs = P("row", "col")
    return jax.shard_map(body, mesh=mesh, in_specs=in_specs, out_specs=out_specs, check_vma=False)
```

time: 430 us -> 103 us (0.24)
  the two profiles are of different devices: /device:TPU:4 before, /device:TPU:6 now
where the time goes in v1:
time: 103 us
  Pallas kernels  101 us (98%)
  local copies, waits for them, and re-layouts  2.04 us (2%)
    pallas_call x1, Pallas kernels, body(): pl.pallas_call(kernel, out_shape=jax.ShapeDtypeStruct((BS, WIDE), jnp.flo...  101 us

profile of v1, /device:TPU:6, one launch (start us, length us, event | category | flops | bytes accessed | tf_op | source)
XLA Modules:
  0.0 103.2 jit_solution(2189747598094136192)
XLA Ops:
  0.0 0.0 copy-start
  0.0 0.8 copy-done
  0.8 0.0 copy-start.1
  0.8 0.7 copy-done.1
  1.4 101.2 %shard_map.28 = f32[64,256]{1,0:T(8,128)S(1)} custom-call(s32[1,4]{1,0:T(1,128)S(1)} %copy-done.1, bf16[64,256]{1,0:T(8,128)(2,1)S(1)} %copy-done), custom_call_target="tpu_custom_call" | custom-call | tf_op jit(solution)/shard_map/pallas_call | solution.py:168
  102.6 0.6 copy.4
Async XLA Ops:
  0.0 0.8 copy-start
  0.8 0.7 copy-start.1

commit v2 on v0

v2 whole, which is shorter than its diff:
```python
import jax
import jax.numpy as jnp
from jax import lax
from jax.experimental import pallas as pl
from jax.experimental.pallas import tpu as pltpu
from jax.sharding import PartitionSpec as P

MESH = pl.DeviceIdType.MESH
NX, NY, NZL, NZH, NC = 4, 4, 8, 4, 2
NZ = NZL * NZH
BS = 64
WIDE = 256
ORDER = 4096

P1, P2, P3, P4 = 0, 1, 2, 3
ROW_L, ROW_R, ROW_LF, ROW_RF = 4, 5, 6, 7
ROW_Y0, ROW_Y1, ROW_Y2 = 8, 9, 10
COL_NEAR, COL_FAR, X_NEAR, X_FAR, C_NEAR, C_FAR = 11, 12, 13, 14, 15, 16
F_1, F_2, F_Y0, F_Y1, F_Y2 = 17, 18, 19, 20, 21
N_SEM = 22


def kernel(flag_ref, h_ref, out_ref, panel, rowp, firstp, xpanel, p1, p2, p3, p4, send, recv):
    row = lax.axis_index("row")
    col = lax.axis_index("col")
    x = lax.div(row, NZL * NC)
    zl = lax.rem(lax.div(row, NC), NZL)
    c = lax.rem(row, NC)
    y = lax.div(col, NZH)
    zh = lax.rem(col, NZH)
    z = zh * NZL + zl
    near = lax.div(zl, 4) * 4
    far = 4 - near
    left = lax.rem(zh + 3, NZH)
    right = lax.rem(zh + 1, NZH)
    across = lax.rem(zh + 2, NZH)

    def dev(x=x, y=y, zl=zl, zh=zh, c=c):
        return ((x * NZL + zl) * NC + c, y * NZH + zh)

    def z_peer(d):
        at = lax.rem(z + d + NZ, NZ)
        return dev(zl=lax.rem(at, NZL), zh=lax.div(at, NZL))

    def x_peer(d):
        return dev(x=lax.rem(x + d, NX))

    def y_peer(d):
        return dev(y=lax.rem(y + d, NY))

    def xc_peer(d):
        at = lax.rem(x * NC + c + d, NX * NC)
        return dev(x=lax.div(at, NC), c=lax.rem(at, NC))

    def put(ref, k, to, dst=None):
        pltpu.make_async_remote_copy(
            src_ref=ref,
            dst_ref=ref if dst is None else dst,
            send_sem=send.at[k],
            recv_sem=recv.at[k],
            device_id=to,
            device_id_type=MESH,
        ).start()

    def take(view, k):
        pltpu.make_async_copy(view, view, recv.at[k]).wait()

    def sent(view, k):
        pltpu.make_async_copy(view, view, send.at[k]).wait()

    barrier = pltpu.get_barrier_semaphore()

    def greet(first, last, peer):
        def step(d, carry):
            pl.semaphore_signal(barrier, inc=1, device_id=peer(d), device_id_type=MESH)
            return carry

        lax.fori_loop(first, last, step, 0)

    greet(1, 9, z_peer)
    greet(-8, 0, z_peer)
    greet(1, NX * NC, xc_peer)
    greet(1, NY, y_peer)

    for b in range(4):
        part = h_ref[:, b * BS:(b + 1) * BS]
        part = jnp.where(flag_ref[0, b] > 0, part, jnp.zeros_like(part))
        panel[x, zl, c, :, b * BS:(b + 1) * BS] = part
        rowp[y, zh, :, b * BS:(b + 1) * BS] = part
    wide = rowp[y, zh].astype(jnp.float32)
    wide = wide * wide
    p1[x * NC + c] = jnp.sum(wide[:, :128] + wide[:, 128:], axis=0, keepdims=True)

    pl.semaphore_wait(barrier, 16 + (NX * NC - 1) + (NY - 1))

    for d in range(1, NX * NC):
        put(p1.at[x * NC + c], P1, xc_peer(d))
    own_row = rowp.at[y, zh]
    put(own_row, ROW_L, dev(zh=right))
    put(own_row, ROW_R, dev(zh=left))
    own_col = panel.at[x, zl, c]
    for d in range(4):
        put(own_col, COL_FAR, dev(zl=far + lax.rem(zl + d, 4)))
    for d in range(1, 4):
        put(own_col, COL_NEAR, dev(zl=near + lax.rem(zl + d, 4)))
    for d in range(1, NY):
        put(own_row, ROW_Y0, y_peer(d))

    take(p1.at[pl.ds(0, 7)], P1)
    p2[y] = jnp.sum(p1[...], axis=0)
    for d in range(1, NY):
        put(p2.at[y], P2, y_peer(d))
    take(p2.at[pl.ds(0, 3)], P2)
    p3[7] = jnp.sum(p2[...], axis=0)
    for d in range(-8, 8):
        if d != 0:
            put(p3.at[7], P3, z_peer(d), p3.at[7 - d])

    take(panel.at[0, pl.ds(0, 3), 0], COL_NEAR)
    batch = panel.at[x, pl.ds(near, 4), c]
    for d in (2, 1, 3):
        put(batch, X_NEAR, x_peer(d))

    half = BS // 2
    take(own_row, ROW_L)
    put(rowp.at[y, left, pl.ds(0, half)], ROW_LF, dev(zh=right))
    take(own_row, ROW_R)
    put(rowp.at[y, right, pl.ds(half, half)], ROW_RF, dev(zh=left))
    for d in range(1, NY):
        put(rowp.at[y, left], ROW_Y1, y_peer(d))
        put(rowp.at[y, right], ROW_Y1, y_peer(d))

    take(panel.at[pl.ds(0, 3), pl.ds(0, 4), 0], X_NEAR)
    put(panel.at[:, pl.ds(near, 4), c], C_NEAR, dev(c=1 - c))
    take(panel.at[0, pl.ds(0, 4), 0], COL_FAR)
    batch = panel.at[x, pl.ds(far, 4), c]
    for d in (2, 1, 3):
        put(batch, X_FAR, x_peer(d))

    take(p3.at[pl.ds(0, 15)], P3)
    p4[2] = jnp.sum(p3[...], axis=0)
    put(p4.at[2], P4, dev(zh=right), p4.at[0])
    put(p4.at[2], P4, dev(zh=left), p4.at[1])

    take(rowp.at[0, 0, pl.ds(0, half)], ROW_LF)
    take(rowp.at[0, 0, pl.ds(0, half)], ROW_RF)
    for d in range(1, NY):
        put(rowp.at[y, across], ROW_Y2, y_peer(d))

    take(panel.at[pl.ds(0, 3), pl.ds(0, 4), 0], X_FAR)
    put(panel.at[:, pl.ds(far, 4), c], C_FAR, dev(c=1 - c))
    take(p4.at[pl.ds(0, 2)], P4)
    squares = jnp.sum(p4[0] + p4[1], axis=1, keepdims=True)
    factor = jnp.sqrt(jnp.float32(ORDER) / squares)
    take(panel.at[:, pl.ds(0, 4), 0], C_NEAR)
    take(panel.at[:, pl.ds(0, 4), 0], C_FAR)
    take(rowp.at[0, pl.ds(0, 3)], ROW_Y0)
    take(rowp.at[pl.ds(0, 3), pl.ds(0, 2)], ROW_Y1)
    take(rowp.at[0, pl.ds(0, 3)], ROW_Y2)

    acc = jnp.zeros((BS, WIDE), jnp.float32)
    for j in range(16):
        lhs = (rowp[j // 4, j % 4].astype(jnp.float32) * factor).astype(jnp.bfloat16)
        rhs = panel[j // 4, (j % 4) * 2:(j % 4) * 2 + 2].reshape(WIDE, WIDE)
        rhs = (rhs.astype(jnp.float32) * factor).astype(jnp.bfloat16)
        xpanel[j] = rhs
        acc += jnp.dot(lhs, rhs, preferred_element_type=jnp.float32)
    firstp[y, zh] = acc.astype(jnp.bfloat16)

    own_first = firstp.at[y, zh]
    put(own_first, F_2, dev(zh=across))
    put(own_first, F_1, dev(zh=right))
    put(own_first, F_1, dev(zh=left))
    for d in range(1, NY):
        put(own_first, F_Y0, y_peer(d))

    def dots(h):
        total = jnp.zeros((BS, WIDE), jnp.float32)
        for i in range(NY):
            total += jnp.dot(firstp[i, h], xpanel[i * NZH + h], preferred_element_type=jnp.float32)
        return total

    take(firstp.at[0, pl.ds(0, 3)], F_Y0)
    acc = dots(zh)
    take(firstp.at[0, pl.ds(0, 2)], F_1)
    for d in range(1, NY):
        put(firstp.at[y, left], F_Y1, y_peer(d))
        put(firstp.at[y, right], F_Y1, y_peer(d))
    take(firstp.at[pl.ds(0, 3), pl.ds(0, 2)], F_Y1)
    acc += dots(left) + dots(right)
    take(own_first, F_2)
    for d in range(1, NY):
        put(firstp.at[y, across], F_Y2, y_peer(d))
    own = (rowp[y, zh].astype(jnp.float32) * factor).astype(jnp.bfloat16).astype(jnp.float32)
    acc = 1.5 * own - 0.5 * acc
    take(firstp.at[0, pl.ds(0, 3)], F_Y2)
    out_ref[...] = 16.0 * (acc - 0.5 * dots(across))

    sent(p1.at[pl.ds(0, 7)], P1)
    sent(p2.at[pl.ds(0, 3)], P2)
    sent(p3.at[pl.ds(0, 15)], P3)
    sent(p4.at[pl.ds(0, 2)], P4)
    sent(own_row, ROW_L)
    sent(own_row, ROW_R)
    sent(rowp.at[0, 0, pl.ds(0, half)], ROW_LF)
    sent(rowp.at[0, 0, pl.ds(0, half)], ROW_RF)
    sent(rowp.at[0, pl.ds(0, 3)], ROW_Y0)
    sent(rowp.at[pl.ds(0, 3), pl.ds(0, 2)], ROW_Y1)
    sent(rowp.at[0, pl.ds(0, 3)], ROW_Y2)
    sent(panel.at[0, pl.ds(0, 3), 0], COL_NEAR)
    sent(panel.at[0, pl.ds(0, 4), 0], COL_FAR)
    sent(panel.at[pl.ds(0, 3), pl.ds(0, 4), 0], X_NEAR)
    sent(panel.at[pl.ds(0, 3), pl.ds(0, 4), 0], X_FAR)
    sent(panel.at[:, pl.ds(0, 4), 0], C_NEAR)
    sent(panel.at[:, pl.ds(0, 4), 0], C_FAR)
    sent(firstp.at[0, pl.ds(0, 2)], F_1)
    sent(own_first, F_2)
    sent(firstp.at[0, pl.ds(0, 3)], F_Y0)
    sent(firstp.at[pl.ds(0, 3), pl.ds(0, 2)], F_Y1)
    sent(firstp.at[0, pl.ds(0, 3)], F_Y2)


SCRATCH = [
    pltpu.VMEM((NX, NZL, NC, BS, WIDE), jnp.bfloat16),
    pltpu.VMEM((NY, NZH, BS, WIDE), jnp.bfloat16),
    pltpu.VMEM((NY, NZH, BS, WIDE), jnp.bfloat16),
    pltpu.VMEM((16, WIDE, WIDE), jnp.bfloat16),
    pltpu.VMEM((NX * NC, 1, 128), jnp.float32),
    pltpu.VMEM((NY, 1, 128), jnp.float32),
    pltpu.VMEM((16, 1, 128), jnp.float32),
    pltpu.VMEM((3, 1, 128), jnp.float32),
    pltpu.SemaphoreType.DMA((N_SEM,)),
    pltpu.SemaphoreType.DMA((N_SEM,)),
]


def body(hamilton, block_flags):
    return pl.pallas_call(
        kernel,
        out_shape=jax.ShapeDtypeStruct((BS, WIDE), jnp.float32),
        in_specs=[
            pl.BlockSpec(memory_space=pltpu.SMEM),
            pl.BlockSpec(memory_space=pltpu.VMEM),
        ],
        out_specs=pl.BlockSpec(memory_space=pltpu.VMEM),
        scratch_shapes=SCRATCH,
        compiler_params=pltpu.CompilerParams(
            collective_id=0, has_side_effects=True, vmem_limit_bytes=32 * 1024 * 1024
        ),
    )(block_flags, hamilton)


def solution(mesh):
    in_specs = (P("row", "col"), P("row", "col"))
    out_specs = P("row", "col")
    return jax.shard_map(body, mesh=mesh, in_specs=in_specs, out_specs=out_specs, check_vma=False)
```

time: 430 us -> 85.3 us (0.20)
  the two profiles are of different devices: /device:TPU:4 before, /device:TPU:64 now
where the time goes in v2:
time: 85.3 us; the launch traced here: 85.1 us
  Pallas kernels  83 us (97%)
  local copies, waits for them, and re-layouts  2.04 us (2%)
    pallas_call x1, Pallas kernels, body(): pl.pallas_call(kernel, out_shape=jax.ShapeDtypeStruct((BS, WIDE), jnp.flo...  83 us
    unnamed x5, local copies, waits for them, and re-layouts  2.04 us

profile of v2, /device:TPU:64, one launch (start us, length us, event | category | flops | bytes accessed | tf_op | source)
XLA Modules:
  0.0 85.1 jit_solution(11942472415711411732)
XLA Ops:
  0.0 0.0 copy-start
  0.0 0.8 copy-done
  0.8 0.0 copy-start.1
  0.8 0.7 copy-done.1
  1.4 83.0 %shard_map.28 = f32[64,256]{1,0:T(8,128)S(1)} custom-call(s32[1,4]{1,0:T(1,128)S(1)} %copy-done.1, bf16[64,256]{1,0:T(8,128)(2,1)S(1)} %copy-done), custom_call_target="tpu_custom_call" | custom-call | tf_op jit(solution)/shard_map/pallas_call | solution.py:238
  84.4 0.6 copy.4
Async XLA Ops:
  0.0 0.8 copy-start
  0.8 0.7 copy-start.1

commit v3 on v2

v3 whole, which is shorter than its diff:
```python
import jax
import jax.numpy as jnp
from jax import lax
from jax.experimental import pallas as pl
from jax.experimental.pallas import tpu as pltpu
from jax.sharding import PartitionSpec as P

MESH = pl.DeviceIdType.MESH
NX, NY, NZL, NZH, NC = 4, 4, 8, 4, 2
NZ = NZL * NZH
BS = 64
WIDE = 256
HALF = 128
ORDER = 4096

P1, P2, P3, P4 = 0, 1, 2, 3
ROW_P, ROW_L, ROW_R, ROW_LF, ROW_RF, ROW_Y0, ROW_Y1, ROW_Y2 = 4, 5, 6, 7, 8, 9, 10, 11
COL = 12
ADD1 = 18
FIRST = 19
ADD2 = 25
N_SEM = 26


def kernel(flag_hbm, h_hbm, out_ref, flag_ref, h_ref, mine, panel, rowp, firstp, xrow, part, got,
           p1, p2, p3, p4, local, send, recv):
    row = lax.axis_index("row")
    col = lax.axis_index("col")
    x = lax.div(row, NZL * NC)
    zl = lax.rem(lax.div(row, NC), NZL)
    c = lax.rem(row, NC)
    y = lax.div(col, NZH)
    zh = lax.rem(col, NZH)
    z = zh * NZL + zl
    p = lax.rem(zl, 2)
    hz = lax.div(zl, 2)
    near = lax.div(hz, 2) * 2
    far = 2 - near
    side = 1 - 2 * p
    left = lax.rem(zh + 3, NZH)
    right = lax.rem(zh + 1, NZH)
    across = lax.rem(zh + 2, NZH)

    def dev(x=x, y=y, zl=zl, zh=zh, c=c):
        return ((x * NZL + zl) * NC + c, y * NZH + zh)

    def z_peer(d):
        at = lax.rem(z + d + NZ, NZ)
        return dev(zl=lax.rem(at, NZL), zh=lax.div(at, NZL))

    def x_peer(d):
        return dev(x=lax.rem(x + d, NX))

    def y_peer(d):
        return dev(y=lax.rem(y + d, NY))

    def xc_peer(d):
        at = lax.rem(x * NC + c + d, NX * NC)
        return dev(x=lax.div(at, NC), c=lax.rem(at, NC))

    def put(ref, k, to, dst=None):
        pltpu.make_async_remote_copy(
            src_ref=ref,
            dst_ref=ref if dst is None else dst,
            send_sem=send.at[k],
            recv_sem=recv.at[k],
            device_id=to,
            device_id_type=MESH,
        ).start()

    def take(view, k):
        pltpu.make_async_copy(view, view, recv.at[k]).wait()

    def sent(view, k):
        pltpu.make_async_copy(view, view, send.at[k]).wait()

    fetch = pltpu.make_async_copy(h_hbm, h_ref, local.at[0])
    fetch.start()
    fetch_flags = pltpu.make_async_copy(flag_hbm, flag_ref, local.at[1])
    fetch_flags.start()

    barrier = pltpu.get_barrier_semaphore()

    def greet(first, last, peer):
        def step(d, carry):
            pl.semaphore_signal(barrier, inc=1, device_id=peer(d), device_id_type=MESH)
            return carry

        lax.fori_loop(first, last, step, 0)

    pl.semaphore_signal(barrier, inc=1, device_id=z_peer(9 * side), device_id_type=MESH)
    greet(1, 9, z_peer)
    greet(-8, 0, z_peer)
    greet(1, NX * NC, xc_peer)
    greet(1, NY, y_peer)

    fetch.wait()
    fetch_flags.wait()
    for b in range(4):
        block = h_ref[:, b * BS:(b + 1) * BS]
        block = jnp.where(flag_ref[0, b] > 0, block, jnp.zeros_like(block))
        panel[x, hz, c, :, b * BS:(b + 1) * BS] = block
        mine[b // 2, :, (b % 2) * BS:(b % 2 + 1) * BS] = block
    rowp[y, zh, p] = mine[p]
    wide0 = mine[0].astype(jnp.float32)
    wide1 = mine[1].astype(jnp.float32)
    p1[x * NC + c] = jnp.sum(wide0 * wide0 + wide1 * wide1, axis=0, keepdims=True)

    pl.semaphore_wait(barrier, 17 + (NX * NC - 1) + (NY - 1))

    mate = zl + side
    for d in range(1, NX * NC):
        put(p1.at[x * NC + c], P1, xc_peer(d))
    slot = rowp.at[y, zh, p]
    for way, k in ((right, ROW_L), (left, ROW_R)):
        put(mine.at[1 - p], k, dev(zl=mate, zh=way), slot)
        put(mine.at[p], k, dev(zh=way), slot)
    put(mine.at[1 - p], ROW_P, dev(zl=mate), slot)

    def over_z(ref, k):
        own = ref.at[x, hz, c]
        for d in range(2):
            put(own, k + 1, dev(zl=2 * (far + lax.rem(hz + d, 2)) + p))
        put(own, k, dev(zl=2 * (near + lax.rem(hz + 1, 2)) + p))

    def over_x(ref, k, batch):
        take(ref.at[0, pl.ds(0, 1 + batch), 0], k + batch)
        lines = ref.at[x, pl.ds(far if batch else near, 2), c]
        for d in (2, 1, 3):
            put(lines, k + 2 + batch, x_peer(d))

    def over_core(ref, k, batch):
        take(ref.at[pl.ds(0, 3), pl.ds(0, 2), 0], k + 2 + batch)
        put(ref.at[:, pl.ds(far if batch else near, 2), c], k + 4 + batch, dev(c=1 - c))

    def have(ref, k, batch):
        take(ref.at[:, pl.ds(0, 2), 0], k + 4 + batch)

    def settled(ref, k):
        for batch in range(2):
            sent(ref.at[0, pl.ds(0, 1 + batch), 0], k + batch)
            sent(ref.at[pl.ds(0, 3), pl.ds(0, 2), 0], k + 2 + batch)
            sent(ref.at[:, pl.ds(0, 2), 0], k + 4 + batch)

    over_z(panel, COL)

    take(slot, ROW_P)
    for d in range(1, NY):
        put(rowp.at[y, zh], ROW_Y0, y_peer(d))
    take(p1.at[pl.ds(0, 7)], P1)
    p2[y] = jnp.sum(p1[...], axis=0)
    for d in range(1, NY):
        put(p2.at[y], P2, y_peer(d))
    over_x(panel, COL, 0)
    take(p2.at[pl.ds(0, 3)], P2)
    p3[7] = jnp.sum(p2[...], axis=0)
    for d in range(-8, 8):
        if d != 0:
            put(p3.at[7], P3, z_peer(d), p3.at[7 - d])

    over_x(panel, COL, 1)
    over_core(panel, COL, 0)
    take(rowp.at[y, left], ROW_L)
    put(rowp.at[y, left, 0], ROW_LF, dev(zh=right))
    take(rowp.at[y, right], ROW_R)
    put(rowp.at[y, right, 1], ROW_RF, dev(zh=left))
    for d in range(1, NY):
        put(rowp.at[y, left], ROW_Y1, y_peer(d))
        put(rowp.at[y, right], ROW_Y1, y_peer(d))
    over_core(panel, COL, 1)

    take(p3.at[pl.ds(0, 15)], P3)
    p4[2] = jnp.sum(p3[...], axis=0)
    put(p4.at[2], P4, dev(zh=right), p4.at[0])
    put(p4.at[2], P4, dev(zh=left), p4.at[1])

    take(slot, ROW_LF)
    take(slot, ROW_RF)
    for d in range(1, NY):
        put(rowp.at[y, across], ROW_Y2, y_peer(d))

    take(p4.at[pl.ds(0, 2)], P4)
    squares = jnp.sum(p4[0] + p4[1], axis=1, keepdims=True)
    factor = jnp.sqrt(jnp.float32(ORDER) / squares)
    have(panel, COL, 0)
    have(panel, COL, 1)
    take(rowp.at[0, pl.ds(0, 3)], ROW_Y0)
    take(rowp.at[pl.ds(0, 3), pl.ds(0, 2)], ROW_Y1)
    take(rowp.at[0, pl.ds(0, 3)], ROW_Y2)

    def scaled(value):
        return (value.astype(jnp.float32) * factor).astype(jnp.bfloat16)

    acc = jnp.zeros((2 * BS, WIDE), jnp.float32)
    for i in range(NY):
        for h in range(0, NZH, 2):
            lhs = jnp.concatenate([rowp[i, h].reshape(2 * BS, HALF), rowp[i, h + 1].reshape(2 * BS, HALF)], axis=1)
            lhs = scaled(lhs)
            xrow[i, h // 2] = lhs
            rhs = scaled(panel[i, h:h + 2].reshape(WIDE, WIDE))
            acc += jnp.dot(lhs, rhs, preferred_element_type=jnp.float32)
    part[...] = acc.reshape(2, BS, WIDE)
    put(part.at[1 - p], ADD1, dev(zl=mate), got.at[0])
    own = scaled(panel[x, hz, c]).astype(jnp.float32)
    take(got.at[0], ADD1)
    firstp[x, hz, c] = (part[p] + got[0]).astype(jnp.bfloat16)

    over_z(firstp, FIRST)
    over_x(firstp, FIRST, 0)
    over_x(firstp, FIRST, 1)
    over_core(firstp, FIRST, 0)
    over_core(firstp, FIRST, 1)
    have(firstp, FIRST, 0)
    sent(part.at[0], ADD1)
    have(firstp, FIRST, 1)

    acc = jnp.zeros((2 * BS, WIDE), jnp.float32)
    for i in range(NY):
        for h in range(0, NZH, 2):
            rhs = firstp[i, h:h + 2].reshape(WIDE, WIDE)
            acc += jnp.dot(xrow[i, h // 2], rhs, preferred_element_type=jnp.float32)
    part[...] = acc.reshape(2, BS, WIDE)
    put(part.at[1 - p], ADD2, dev(zl=mate), got.at[1])
    settled(panel, COL)
    settled(firstp, FIRST)
    sent(p1.at[pl.ds(0, 7)], P1)
    sent(p2.at[pl.ds(0, 3)], P2)
    sent(p3.at[pl.ds(0, 15)], P3)
    sent(p4.at[pl.ds(0, 2)], P4)
    sent(slot, ROW_P)
    sent(rowp.at[0, 0], ROW_L)
    sent(rowp.at[0, 0], ROW_R)
    sent(slot, ROW_LF)
    sent(slot, ROW_RF)
    sent(rowp.at[0, pl.ds(0, 3)], ROW_Y0)
    sent(rowp.at[pl.ds(0, 3), pl.ds(0, 2)], ROW_Y1)
    sent(rowp.at[0, pl.ds(0, 3)], ROW_Y2)
    take(got.at[1], ADD2)
    out_ref[...] = 16.0 * (1.5 * own - 0.5 * (part[p] + got[1]))
    sent(part.at[0], ADD2)


SCRATCH = [
    pltpu.SMEM((1, 4), jnp.int32),
    pltpu.VMEM((BS, WIDE), jnp.bfloat16),
    pltpu.VMEM((2, BS, HALF), jnp.bfloat16),
    pltpu.VMEM((NX, NZH, NC, BS, WIDE), jnp.bfloat16),
    pltpu.VMEM((NY, NZH, 2, BS, HALF), jnp.bfloat16),
    pltpu.VMEM((NX, NZH, NC, BS, WIDE), jnp.bfloat16),
    pltpu.VMEM((NY, 2, 2 * BS, WIDE), jnp.bfloat16),
    pltpu.VMEM((2, BS, WIDE), jnp.float32),
    pltpu.VMEM((2, BS, WIDE), jnp.float32),
    pltpu.VMEM((NX * NC, 1, 128), jnp.float32),
    pltpu.VMEM((NY, 1, 128), jnp.float32),
    pltpu.VMEM((16, 1, 128), jnp.float32),
    pltpu.VMEM((3, 1, 128), jnp.float32),
    pltpu.SemaphoreType.DMA((2,)),
    pltpu.SemaphoreType.DMA((N_SEM,)),
    pltpu.SemaphoreType.DMA((N_SEM,)),
]


def body(hamilton, block_flags):
    return pl.pallas_call(
        kernel,
        out_shape=jax.ShapeDtypeStruct((BS, WIDE), jnp.float32),
        in_specs=[pl.BlockSpec(memory_space=pl.ANY)] * 2,
        out_specs=pl.BlockSpec(memory_space=pltpu.VMEM),
        scratch_shapes=SCRATCH,
        compiler_params=pltpu.CompilerParams(collective_id=0, has_side_effects=True),
    )(block_flags, hamilton)


def solution(mesh):
    in_specs = (P("row", "col"), P("row", "col"))
    out_specs = P("row", "col")
    return jax.shard_map(body, mesh=mesh, in_specs=in_specs, out_specs=out_specs, check_vma=False)
```

time: 85.3 us -> 75.9 us (0.89)
  the two profiles are of different devices: /device:TPU:64 before, /device:TPU:1 now
where the time goes in v3:
time: 75.9 us; the launch traced here: 75.6 us
  Pallas kernels  74.2 us (98%)
  local copies, waits for them, and re-layouts  1.47 us (2%)
    pallas_call x1, Pallas kernels, body(): pl.pallas_call(kernel, out_shape=jax.ShapeDtypeStruct((BS, WIDE), jnp.flo...  74.2 us

profile of v3, /device:TPU:1, one launch (start us, length us, event | category | flops | bytes accessed | tf_op | source)
XLA Modules:
  0.0 75.6 jit_solution(11092297491956430753)
XLA Ops:
  0.0 74.2 %shard_map.28 = f32[64,256]{1,0:T(8,128)} custom-call(s32[1,4]{1,0:T(1,128)} %flag_hbm.1, bf16[64,256]{1,0:T(8,128)(2,1)} %h_hbm.1), custom_call_target="tpu_custom_call" | custom-call | tf_op jit(solution)/shard_map/pallas_call | solution.py:264
  74.2 1.5 %copy.4 = f32[64,256]{1,0:T(8,128)} copy(f32[64,256]{1,0:T(8,128)} %shard_map.28) | data formatting | bytes 131072

commit v4 on v3

--- a/solution.py
+++ b/solution.py
@@ -13,8 +13,10 @@
 HALF = 128
 ORDER = 4096
 
+LEFT, OWN, RIGHT, ACROSS = 0, 1, 2, 3
+
 P1, P2, P3, P4 = 0, 1, 2, 3
-ROW_P, ROW_L, ROW_R, ROW_LF, ROW_RF, ROW_Y0, ROW_Y1, ROW_Y2 = 4, 5, 6, 7, 8, 9, 10, 11
+ROW_P, ROW_L, ROW_R, ROW_LF, ROW_RF, ROW_Y1, ROW_Y2 = 4, 5, 6, 7, 8, 9, 10
 COL = 12
 ADD1 = 18
 FIRST = 19
@@ -39,7 +41,6 @@
     side = 1 - 2 * p
     left = lax.rem(zh + 3, NZH)
     right = lax.rem(zh + 1, NZH)
-    across = lax.rem(zh + 2, NZH)
 
     def dev(x=x, y=y, zl=zl, zh=zh, c=c):
         return ((x * NZL + zl) * NC + c, y * NZH + zh)
@@ -101,7 +102,7 @@
         block = jnp.where(flag_ref[0, b] > 0, block, jnp.zeros_like(block))
         panel[x, hz, c, :, b * BS:(b + 1) * BS] = block
         mine[b // 2, :, (b % 2) * BS:(b % 2 + 1) * BS] = block
-    rowp[y, zh, p] = mine[p]
+    rowp[y, OWN, p] = mine[p]
     wide0 = mine[0].astype(jnp.float32)
     wide1 = mine[1].astype(jnp.float32)
     p1[x * NC + c] = jnp.sum(wide0 * wide0 + wide1 * wide1, axis=0, keepdims=True)
@@ -111,11 +112,10 @@
     mate = zl + side
     for d in range(1, NX * NC):
         put(p1.at[x * NC + c], P1, xc_peer(d))
-    slot = rowp.at[y, zh, p]
-    for way, k in ((right, ROW_L), (left, ROW_R)):
-        put(mine.at[1 - p], k, dev(zl=mate, zh=way), slot)
-        put(mine.at[p], k, dev(zh=way), slot)
-    put(mine.at[1 - p], ROW_P, dev(zl=mate), slot)
+    for way, k, at in ((right, ROW_L, LEFT), (left, ROW_R, RIGHT)):
+        put(mine.at[1 - p], k, dev(zl=mate, zh=way), rowp.at[y, at, p])
+        put(mine.at[p], k, dev(zh=way), rowp.at[y, at, p])
+    put(mine.at[1 - p], ROW_P, dev(zl=mate), rowp.at[y, OWN, p])
 
     def over_z(ref, k):
         own = ref.at[x, hz, c]
@@ -144,52 +144,52 @@
 
     over_z(panel, COL)
 
-    take(slot, ROW_P)
-    for d in range(1, NY):
-        put(rowp.at[y, zh], ROW_Y0, y_peer(d))
     take(p1.at[pl.ds(0, 7)], P1)
     p2[y] = jnp.sum(p1[...], axis=0)
     for d in range(1, NY):
         put(p2.at[y], P2, y_peer(d))
-    over_x(panel, COL, 0)
     take(p2.at[pl.ds(0, 3)], P2)
     p3[7] = jnp.sum(p2[...], axis=0)
     for d in range(-8, 8):
         if d != 0:
             put(p3.at[7], P3, z_peer(d), p3.at[7 - d])
 
+    over_x(panel, COL, 0)
+    take(rowp.at[y, LEFT], ROW_L)
+    put(rowp.at[y, LEFT, 0], ROW_LF, dev(zh=right), rowp.at[y, ACROSS, 0])
+    take(rowp.at[y, RIGHT], ROW_R)
+    put(rowp.at[y, RIGHT, 1], ROW_RF, dev(zh=left), rowp.at[y, ACROSS, 1])
+    take(rowp.at[y, OWN, 0], ROW_P)
+    for d in (2, 1, 3):
+        put(rowp.at[y, pl.ds(0, 3)], ROW_Y1, y_peer(d))
     over_x(panel, COL, 1)
     over_core(panel, COL, 0)
-    take(rowp.at[y, left], ROW_L)
-    put(rowp.at[y, left, 0], ROW_LF, dev(zh=right))
-    take(rowp.at[y, right], ROW_R)
-    put(rowp.at[y, right, 1], ROW_RF, dev(zh=left))
-    for d in range(1, NY):
-        put(rowp.at[y, left], ROW_Y1, y_peer(d))
-        put(rowp.at[y, right], ROW_Y1, y_peer(d))
-    over_core(panel, COL, 1)
-
     take(p3.at[pl.ds(0, 15)], P3)
     p4[2] = jnp.sum(p3[...], axis=0)
     put(p4.at[2], P4, dev(zh=right), p4.at[0])
     put(p4.at[2], P4, dev(zh=left), p4.at[1])
 
-    take(slot, ROW_LF)
-    take(slot, ROW_RF)
-    for d in range(1, NY):
-        put(rowp.at[y, across], ROW_Y2, y_peer(d))
+    over_core(panel, COL, 1)
+
+    take(rowp.at[y, ACROSS, 0], ROW_LF)
+    take(rowp.at[y, ACROSS, 1], ROW_RF)
+    for d in (2, 1, 3):
+        put(rowp.at[y, ACROSS], ROW_Y2, y_peer(d))
 
     take(p4.at[pl.ds(0, 2)], P4)
     squares = jnp.sum(p4[0] + p4[1], axis=1, keepdims=True)
     factor = jnp.sqrt(jnp.float32(ORDER) / squares)
     have(panel, COL, 0)
     have(panel, COL, 1)
-    take(rowp.at[0, pl.ds(0, 3)], ROW_Y0)
-    take(rowp.at[pl.ds(0, 3), pl.ds(0, 2)], ROW_Y1)
+    take(rowp.at[pl.ds(0, 3), pl.ds(0, 3)], ROW_Y1)
     take(rowp.at[0, pl.ds(0, 3)], ROW_Y2)
 
     def scaled(value):
         return (value.astype(jnp.float32) * factor).astype(jnp.bfloat16)
+
+    def deep(ref, i, h):
+        parts = [ref[i, lax.rem(zh + 3 + at, NZH)].reshape(2 * BS, WIDE) for at in (h, h + 1)]
+        return jnp.concatenate(parts, axis=0)
 
     acc = jnp.zeros((2 * BS, WIDE), jnp.float32)
     for i in range(NY):
@@ -197,7 +197,7 @@
             lhs = jnp.concatenate([rowp[i, h].reshape(2 * BS, HALF), rowp[i, h + 1].reshape(2 * BS, HALF)], axis=1)
             lhs = scaled(lhs)
             xrow[i, h // 2] = lhs
-            rhs = scaled(panel[i, h:h + 2].reshape(WIDE, WIDE))
+            rhs = scaled(deep(panel, i, h))
             acc += jnp.dot(lhs, rhs, preferred_element_type=jnp.float32)
     part[...] = acc.reshape(2, BS, WIDE)
     put(part.at[1 - p], ADD1, dev(zl=mate), got.at[0])
@@ -217,7 +217,7 @@
     acc = jnp.zeros((2 * BS, WIDE), jnp.float32)
     for i in range(NY):
         for h in range(0, NZH, 2):
-            rhs = firstp[i, h:h + 2].reshape(WIDE, WIDE)
+            rhs = deep(firstp, i, h)
             acc += jnp.dot(xrow[i, h // 2], rhs, preferred_element_type=jnp.float32)
     part[...] = acc.reshape(2, BS, WIDE)
     put(part.at[1 - p], ADD2, dev(zl=mate), got.at[1])
@@ -227,13 +227,12 @@
     sent(p2.at[pl.ds(0, 3)], P2)
     sent(p3.at[pl.ds(0, 15)], P3)
     sent(p4.at[pl.ds(0, 2)], P4)
-    sent(slot, ROW_P)
+    sent(mine.at[0], ROW_P)
     sent(rowp.at[0, 0], ROW_L)
     sent(rowp.at[0, 0], ROW_R)
-    sent(slot, ROW_LF)
-    sent(slot, ROW_RF)
-    sent(rowp.at[0, pl.ds(0, 3)], ROW_Y0)
-    sent(rowp.at[pl.ds(0, 3), pl.ds(0, 2)], ROW_Y1)
+    sent(mine.at[0], ROW_LF)
+    sent(mine.at[0], ROW_RF)
+    sent(rowp.at[pl.ds(0, 3), pl.ds(0, 3)], ROW_Y1)
     sent(rowp.at[0, pl.ds(0, 3)], ROW_Y2)
     take(got.at[1], ADD2)
     out_ref[...] = 16.0 * (1.5 * own - 0.5 * (part[p] + got[1]))

time: 75.9 us -> 73 us (0.962)
  Pallas kernels: 74.2 us -> 71.2 us
    pallas_call x1, Pallas kernels: 74.2 us -> 71.2 us  [body(): pl.pallas_call(kernel, out_shape=jax.ShapeDtypeStruct((BS, WIDE), jnp.flo...]
where the time goes in v4:
time: 73 us; the launch traced here: 72.7 us
  Pallas kernels  71.2 us (98%)
  local copies, waits for them, and re-layouts  1.47 us (2%)
    pallas_call x1, Pallas kernels, body(): pl.pallas_call(kernel, out_shape=jax.ShapeDtypeStruct((BS, WIDE), jnp.flo...  71.2 us
    unnamed x1, local copies, waits for them, and re-layouts  1.47 us

profile of v4, /device:TPU:1, one launch (start us, length us, event | category | flops | bytes accessed | tf_op | source)
XLA Modules:
  0.0 72.7 jit_solution(9780386431321623280)
XLA Ops:
  0.0 71.2 %shard_map.28 = f32[64,256]{1,0:T(8,128)} custom-call(s32[1,4]{1,0:T(1,128)} %flag_hbm.1, bf16[64,256]{1,0:T(8,128)(2,1)} %h_hbm.1), custom_call_target="tpu_custom_call" | custom-call | tf_op jit(solution)/shard_map/pallas_call | solution.py:263
  71.2 1.5 %copy.4 = f32[64,256]{1,0:T(8,128)} copy(f32[64,256]{1,0:T(8,128)} %shard_map.28) | data formatting | bytes 131072

commit v5 on v4

--- a/solution.py
+++ b/solution.py
@@ -24,7 +24,7 @@
 N_SEM = 26
 
 
-def kernel(flag_hbm, h_hbm, out_ref, flag_ref, h_ref, mine, panel, rowp, firstp, xrow, part, got,
+def kernel(flag_hbm, h_hbm, out_ref, flag_ref, h_ref, mine, panel, rowp, firstp, xrow, xpanel, part, got,
            p1, p2, p3, p4, local, send, recv):
     row = lax.axis_index("row")
     col = lax.axis_index("col")
@@ -119,9 +119,9 @@
 
     def over_z(ref, k):
         own = ref.at[x, hz, c]
+        put(own, k, dev(zl=2 * (near + lax.rem(hz + 1, 2)) + p))
         for d in range(2):
             put(own, k + 1, dev(zl=2 * (far + lax.rem(hz + d, 2)) + p))
-        put(own, k, dev(zl=2 * (near + lax.rem(hz + 1, 2)) + p))
 
     def over_x(ref, k, batch):
         take(ref.at[0, pl.ds(0, 1 + batch), 0], k + batch)
@@ -191,19 +191,32 @@
         parts = [ref[i, lax.rem(zh + 3 + at, NZH)].reshape(2 * BS, WIDE) for at in (h, h + 1)]
         return jnp.concatenate(parts, axis=0)
 
-    acc = jnp.zeros((2 * BS, WIDE), jnp.float32)
-    for i in range(NY):
-        for h in range(0, NZH, 2):
-            lhs = jnp.concatenate([rowp[i, h].reshape(2 * BS, HALF), rowp[i, h + 1].reshape(2 * BS, HALF)], axis=1)
-            lhs = scaled(lhs)
-            xrow[i, h // 2] = lhs
-            rhs = scaled(deep(panel, i, h))
-            acc += jnp.dot(lhs, rhs, preferred_element_type=jnp.float32)
-    part[...] = acc.reshape(2, BS, WIDE)
-    put(part.at[1 - p], ADD1, dev(zl=mate), got.at[0])
+    def product(rows, columns):
+        acc = jnp.zeros((BS, WIDE), jnp.float32)
+        for i in range(NY):
+            for h in range(0, NZH, 2):
+                acc += jnp.dot(rows(i, h), columns(i, h), preferred_element_type=jnp.float32)
+        return acc
+
+    def fresh(at):
+        def rows(i, h):
+            lhs = scaled(jnp.concatenate([rowp[i, h, at], rowp[i, h + 1, at]], axis=1))
+            xrow[i, h // 2, at] = lhs
+            return lhs
+
+        return rows
+
+    def fresh_columns(i, h):
+        rhs = scaled(deep(panel, i, h))
+        xpanel[i, h // 2] = rhs
+        return rhs
+
+    part[0] = product(fresh(1 - p), fresh_columns)
+    put(part.at[0], ADD1, dev(zl=mate), got.at[0])
+    mid = product(fresh(p), lambda i, h: xpanel[i, h // 2])
     own = scaled(panel[x, hz, c]).astype(jnp.float32)
     take(got.at[0], ADD1)
-    firstp[x, hz, c] = (part[p] + got[0]).astype(jnp.bfloat16)
+    firstp[x, hz, c] = (mid + got[0]).astype(jnp.bfloat16)
 
     over_z(firstp, FIRST)
     over_x(firstp, FIRST, 0)
@@ -214,13 +227,10 @@
     sent(part.at[0], ADD1)
     have(firstp, FIRST, 1)
 
-    acc = jnp.zeros((2 * BS, WIDE), jnp.float32)
-    for i in range(NY):
-        for h in range(0, NZH, 2):
-            rhs = deep(firstp, i, h)
-            acc += jnp.dot(xrow[i, h // 2], rhs, preferred_element_type=jnp.float32)
-    part[...] = acc.reshape(2, BS, WIDE)
-    put(part.at[1 - p], ADD2, dev(zl=mate), got.at[1])
+    part[1] = product(lambda i, h: xrow[i, h // 2, 1 - p], lambda i, h: deep(firstp, i, h))
+    put(part.at[1], ADD2, dev(zl=mate), got.at[1])
+    last = product(lambda i, h: xrow[i, h // 2, p], lambda i, h: deep(firstp, i, h))
+    last = 1.5 * own - 0.5 * last
     settled(panel, COL)
     settled(firstp, FIRST)
     sent(p1.at[pl.ds(0, 7)], P1)
@@ -235,7 +245,7 @@
     sent(rowp.at[pl.ds(0, 3), pl.ds(0, 3)], ROW_Y1)
     sent(rowp.at[0, pl.ds(0, 3)], ROW_Y2)
     take(got.at[1], ADD2)
-    out_ref[...] = 16.0 * (1.5 * own - 0.5 * (part[p] + got[1]))
+    out_ref[...] = 16.0 * (last - 0.5 * got[1])
     sent(part.at[0], ADD2)
 
 
@@ -246,7 +256,8 @@
     pltpu.VMEM((NX, NZH, NC, BS, WIDE), jnp.bfloat16),
     pltpu.VMEM((NY, NZH, 2, BS, HALF), jnp.bfloat16),
     pltpu.VMEM((NX, NZH, NC, BS, WIDE), jnp.bfloat16),
-    pltpu.VMEM((NY, 2, 2 * BS, WIDE), jnp.bfloat16),
+    pltpu.VMEM((NY, 2, 2, BS, WIDE), jnp.bfloat16),
+    pltpu.VMEM((NY, 2, WIDE, WIDE), jnp.bfloat16),
     pltpu.VMEM((2, BS, WIDE), jnp.float32),
     pltpu.VMEM((2, BS, WIDE), jnp.float32),
     pltpu.VMEM((NX * NC, 1, 128), jnp.float32),
@@ -266,7 +277,7 @@
         in_specs=[pl.BlockSpec(memory_space=pl.ANY)] * 2,
         out_specs=pl.BlockSpec(memory_space=pltpu.VMEM),
         scratch_shapes=SCRATCH,
-        compiler_params=pltpu.CompilerParams(collective_id=0, has_side_effects=True),
+        compiler_params=pltpu.CompilerParams(collective_id=0, has_side_effects=True, vmem_limit_bytes=48 * 1024 * 1024),
     )(block_flags, hamilton)
 
 

time: 73 us -> 71.8 us (0.984)
  Pallas kernels: 71.2 us -> 69.5 us
    pallas_call x1, Pallas kernels: 71.2 us -> 69.5 us  [body(): pl.pallas_call(kernel, out_shape=jax.ShapeDtypeStruct((BS, WIDE), jnp.flo...]
    unnamed x1 -> x5, local copies, waits for them, and re-layouts: 1.47 us -> 2.04 us
where the time goes in v5:
time: 71.8 us; the launch traced here: 71.6 us
  Pallas kernels  69.5 us (97%)
  local copies, waits for them, and re-layouts  2.04 us (3%)
    pallas_call x1, Pallas kernels, body(): pl.pallas_call(kernel, out_shape=jax.ShapeDtypeStruct((BS, WIDE), jnp.flo...  69.5 us
    unnamed x5, local copies, waits for them, and re-layouts  2.04 us

profile of v5, /device:TPU:1, one launch (start us, length us, event | category | flops | bytes accessed | tf_op | source)
XLA Modules:
  0.0 71.6 jit_solution(14510860009506960180)
XLA Ops:
  0.0 0.0 copy-start
  0.0 0.8 %copy-done = bf16[64,256]{1,0:T(8,128)(2,1)S(1)} copy-done((bf16[64,256]{1,0:T(8,128)(2,1)S(1)}, bf16[64,256]{1,0:T(8,128)(2,1)}, u32[]{:S(2)}) %copy-start) | copy-done | bytes 32792
  0.8 0.0 copy-start.1
  0.8 0.7 copy-done.1
  1.4 69.5 %shard_map.28 = f32[64,256]{1,0:T(8,128)S(1)} custom-call(s32[1,4]{1,0:T(1,128)S(1)} %copy-done.1, bf16[64,256]{1,0:T(8,128)(2,1)S(1)} %copy-done), custom_call_target="tpu_custom_call" | custom-call | tf_op jit(solution)/shard_map/pallas_call | solution.py:274
  71.0 0.6 copy.4
Async XLA Ops:
  0.0 0.8 %copy-start = (bf16[64,256]{1,0:T(8,128)(2,1)S(1)}, bf16[64,256]{1,0:T(8,128)(2,1)}, u32[]{:S(2)}) copy-start(bf16[64,256]{1,0:T(8,128)(2,1)} %h_hbm.1) | copy-start | bytes 98308
  0.8 0.7 copy-start.1

commit v6 on v5

--- a/solution.py
+++ b/solution.py
@@ -114,6 +114,7 @@
         put(p1.at[x * NC + c], P1, xc_peer(d))
     for way, k, at in ((right, ROW_L, LEFT), (left, ROW_R, RIGHT)):
         put(mine.at[1 - p], k, dev(zl=mate, zh=way), rowp.at[y, at, p])
+    for way, k, at in ((right, ROW_L, LEFT), (left, ROW_R, RIGHT)):
         put(mine.at[p], k, dev(zh=way), rowp.at[y, at, p])
     put(mine.at[1 - p], ROW_P, dev(zl=mate), rowp.at[y, OWN, p])
 
@@ -187,33 +188,36 @@
     def scaled(value):
         return (value.astype(jnp.float32) * factor).astype(jnp.bfloat16)
 
-    def deep(ref, i, h):
-        parts = [ref[i, lax.rem(zh + 3 + at, NZH)].reshape(2 * BS, WIDE) for at in (h, h + 1)]
-        return jnp.concatenate(parts, axis=0)
-
-    def product(rows, columns):
+    starts = (near, far)
+
+    def deep(ref, i, half):
+        return ref[i, pl.ds(starts[half], 2)].reshape(WIDE, WIDE)
+
+    def product(rows, columns, halves=(0, 1)):
         acc = jnp.zeros((BS, WIDE), jnp.float32)
-        for i in range(NY):
-            for h in range(0, NZH, 2):
-                acc += jnp.dot(rows(i, h), columns(i, h), preferred_element_type=jnp.float32)
+        for half in halves:
+            for i in range(NY):
+                acc += jnp.dot(rows(i, half), columns(i, half), preferred_element_type=jnp.float32)
         return acc
 
     def fresh(at):
-        def rows(i, h):
-            lhs = scaled(jnp.concatenate([rowp[i, h, at], rowp[i, h + 1, at]], axis=1))
-            xrow[i, h // 2, at] = lhs
+        def rows(i, half):
+            place = lax.rem(starts[half] - zh + 1 + NZH, NZH)
+            after = lax.rem(place + 1, NZH)
+            lhs = scaled(jnp.concatenate([rowp[i, place, at], rowp[i, after, at]], axis=1))
+            xrow[i, half, at] = lhs
             return lhs
 
         return rows
 
-    def fresh_columns(i, h):
-        rhs = scaled(deep(panel, i, h))
-        xpanel[i, h // 2] = rhs
+    def fresh_columns(i, half):
+        rhs = scaled(deep(panel, i, half))
+        xpanel[i, half] = rhs
         return rhs
 
     part[0] = product(fresh(1 - p), fresh_columns)
     put(part.at[0], ADD1, dev(zl=mate), got.at[0])
-    mid = product(fresh(p), lambda i, h: xpanel[i, h // 2])
+    mid = product(fresh(p), lambda i, half: xpanel[i, half])
     own = scaled(panel[x, hz, c]).astype(jnp.float32)
     take(got.at[0], ADD1)
     firstp[x, hz, c] = (mid + got[0]).astype(jnp.bfloat16)
@@ -223,13 +227,20 @@
     over_x(firstp, FIRST, 1)
     over_core(firstp, FIRST, 0)
     over_core(firstp, FIRST, 1)
+    def kept(at):
+        return lambda i, half: xrow[i, half, at]
+
+    def squared(i, half):
+        return deep(firstp, i, half)
+
     have(firstp, FIRST, 0)
+    part[1] = product(kept(1 - p), squared, (0,))
+    last = product(kept(p), squared, (0,))
     sent(part.at[0], ADD1)
     have(firstp, FIRST, 1)
-
-    part[1] = product(lambda i, h: xrow[i, h // 2, 1 - p], lambda i, h: deep(firstp, i, h))
+    part[1] += product(kept(1 - p), squared, (1,))
     put(part.at[1], ADD2, dev(zl=mate), got.at[1])
-    last = product(lambda i, h: xrow[i, h // 2, p], lambda i, h: deep(firstp, i, h))
+    last += product(kept(p), squared, (1,))
     last = 1.5 * own - 0.5 * last
     settled(panel, COL)
     settled(firstp, FIRST)

time: 71.8 us -> 71.7 us (level)
  no operation moved by 1% of the time
where the time goes in v6:
time: 71.7 us; the launch traced here: 71.4 us
  Pallas kernels  69.4 us (97%)
  local copies, waits for them, and re-layouts  2.04 us (3%)
    pallas_call x1, Pallas kernels, body(): pl.pallas_call(kernel, out_shape=jax.ShapeDtypeStruct((BS, WIDE), jnp.flo...  69.4 us
    unnamed x5, local copies, waits for them, and re-layouts  2.04 us

profile of v6, /device:TPU:1, one launch (start us, length us, event | category | flops | bytes accessed | tf_op | source)
XLA Modules:
  0.0 71.4 jit_solution(5024390171340082559)
XLA Ops:
  0.0 0.0 copy-start
  0.0 0.8 %copy-done = bf16[64,256]{1,0:T(8,128)(2,1)S(1)} copy-done((bf16[64,256]{1,0:T(8,128)(2,1)S(1)}, bf16[64,256]{1,0:T(8,128)(2,1)}, u32[]{:S(2)}) %copy-start) | copy-done | bytes 32792
  0.8 0.0 copy-start.1
  0.8 0.7 copy-done.1
  1.4 69.4 %shard_map.28 = f32[64,256]{1,0:T(8,128)S(1)} custom-call(s32[1,4]{1,0:T(1,128)S(1)} %copy-done.1, bf16[64,256]{1,0:T(8,128)(2,1)S(1)} %copy-done), custom_call_target="tpu_custom_call" | custom-call | tf_op jit(solution)/shard_map/pallas_call | solution.py:285
  70.8 0.6 copy.4
Async XLA Ops:
  0.0 0.8 %copy-start = (bf16[64,256]{1,0:T(8,128)(2,1)S(1)}, bf16[64,256]{1,0:T(8,128)(2,1)}, u32[]{:S(2)}) copy-start(bf16[64,256]{1,0:T(8,128)(2,1)} %h_hbm.1) | copy-start | bytes 98308
  0.8 0.7 copy-start.1

commit v7 on v6

--- a/solution.py
+++ b/solution.py
@@ -164,13 +164,14 @@
     for d in (2, 1, 3):
         put(rowp.at[y, pl.ds(0, 3)], ROW_Y1, y_peer(d))
     over_x(panel, COL, 1)
-    over_core(panel, COL, 0)
     take(p3.at[pl.ds(0, 15)], P3)
     p4[2] = jnp.sum(p3[...], axis=0)
     put(p4.at[2], P4, dev(zh=right), p4.at[0])
     put(p4.at[2], P4, dev(zh=left), p4.at[1])
 
-    over_core(panel, COL, 1)
+    take(panel.at[pl.ds(0, 3), pl.ds(0, 2), 0], COL + 2)
+    take(panel.at[pl.ds(0, 3), pl.ds(0, 2), 0], COL + 3)
+    put(panel.at[:, :, c], COL + 4, dev(c=1 - c))
 
     take(rowp.at[y, ACROSS, 0], ROW_LF)
     take(rowp.at[y, ACROSS, 1], ROW_RF)
@@ -180,8 +181,7 @@
     take(p4.at[pl.ds(0, 2)], P4)
     squares = jnp.sum(p4[0] + p4[1], axis=1, keepdims=True)
     factor = jnp.sqrt(jnp.float32(ORDER) / squares)
-    have(panel, COL, 0)
-    have(panel, COL, 1)
+    take(panel.at[:, :, 0], COL + 4)
     take(rowp.at[pl.ds(0, 3), pl.ds(0, 3)], ROW_Y1)
     take(rowp.at[0, pl.ds(0, 3)], ROW_Y2)
 
@@ -242,7 +242,11 @@
     put(part.at[1], ADD2, dev(zl=mate), got.at[1])
     last += product(kept(p), squared, (1,))
     last = 1.5 * own - 0.5 * last
-    settled(panel, COL)
+    sent(panel.at[0, 0, 0], COL)
+    sent(panel.at[0, pl.ds(0, 2), 0], COL + 1)
+    sent(panel.at[pl.ds(0, 3), pl.ds(0, 2), 0], COL + 2)
+    sent(panel.at[pl.ds(0, 3), pl.ds(0, 2), 0], COL + 3)
+    sent(panel.at[:, :, 0], COL + 4)
     settled(firstp, FIRST)
     sent(p1.at[pl.ds(0, 7)], P1)
     sent(p2.at[pl.ds(0, 3)], P2)

time: 71.7 us -> 71.7 us (level)
  no operation moved by 1% of the time
where the time goes in v7:
time: 71.7 us; the launch traced here: 71.4 us
  Pallas kernels  69.4 us (97%)
  local copies, waits for them, and re-layouts  2.04 us (3%)
    pallas_call x1, Pallas kernels, body(): pl.pallas_call(kernel, out_shape=jax.ShapeDtypeStruct((BS, WIDE), jnp.flo...  69.4 us
    unnamed x5, local copies, waits for them, and re-layouts  2.04 us

profile of v7, /device:TPU:1, one launch (start us, length us, event | category | flops | bytes accessed | tf_op | source)
XLA Modules:
  0.0 71.4 jit_solution(5578755967607522427)
XLA Ops:
  0.0 0.0 copy-start
  0.0 0.8 %copy-done = bf16[64,256]{1,0:T(8,128)(2,1)S(1)} copy-done((bf16[64,256]{1,0:T(8,128)(2,1)S(1)}, bf16[64,256]{1,0:T(8,128)(2,1)}, u32[]{:S(2)}) %copy-start) | copy-done | bytes 32792
  0.8 0.0 copy-start.1
  0.8 0.7 copy-done.1
  1.4 69.4 %shard_map.28 = f32[64,256]{1,0:T(8,128)S(1)} custom-call(s32[1,4]{1,0:T(1,128)S(1)} %copy-done.1, bf16[64,256]{1,0:T(8,128)(2,1)S(1)} %copy-done), custom_call_target="tpu_custom_call" | custom-call | tf_op jit(solution)/shard_map/pallas_call | solution.py:289
  70.8 0.6 copy.4
Async XLA Ops:
  0.0 0.8 %copy-start = (bf16[64,256]{1,0:T(8,128)(2,1)S(1)}, bf16[64,256]{1,0:T(8,128)(2,1)}, u32[]{:S(2)}) copy-start(bf16[64,256]{1,0:T(8,128)(2,1)} %h_hbm.1) | copy-start | bytes 98308
  0.8 0.7 copy-start.1
